TPU v7x, 32 devices: a whole 2x2x4 slice. The times are simulated.
32 devices in a mesh: sub: 4 (over x, core), front: 8 (over z, y).
Axes of the slice: x: 2, y: 2, z: 4, core: 2. Of those that a mesh axis runs over, the one named last changes fastest.
Arguments:
- factor_inverse: bfloat16 [4, 2, 4096, 4096], P('sub', None, 'front'), as said below
- contribution: bfloat16 [4, 2, 4096, 4096], P('sub', None, None, 'front'), may hold values from -0.09375 to 0.09375
- block_map: int32 [4, 2, 32], P('sub'), may hold values from 0 to 31, as said below
- sep_size: int32 [4, 2], P('sub'), may hold values from 1024 to 4096, as said below
- right_side: float32 [4, 2, 4096, 128], P('sub', None, 'front'), may hold values from -6 to 6
Outputs:
- solution: float32 [4, 2, 4096, 128], P('sub', None, 'front')
Inputs may be any that keep to these rules, and one draw needn't show every extreme that they name: `block_map`: for each front the 32 entries are all different. `sep_size`: front (0, 1) always uses all 4096 rows, leaf 4 - 1 uses 4096 // 4. `factor_inverse`: every block is zero above its diagonal.
All inputs are finite; a program needn't handle non-finite values.
Results may differ from a plain program's by a relative error of at most 0.023.
Values may be sent and summed in bfloat16 or wider, within the bound.
A program may use at most 192 MiB of HBM per device.

v0:
```python
import jax
import jax.numpy as jnp
from jax import lax
from jax.sharding import PartitionSpec as P


def shifted(value, axis, steps):
    count = lax.axis_size(axis)
    first, last = (max(0, -steps), min(count, count - steps))
    return lax.ppermute(value, axis, [(source, source + steps) for source in range(first, last)])


def add_columns(inverse, portion):
    return jnp.dot(inverse, portion, preferred_element_type=jnp.float32)


def transpose_term(inverse, source):
    return jnp.einsum("rc,rn->cn", inverse, source, preferred_element_type=jnp.float32)


def place_blocks(block_link, values, first_block, count_blocks, block_rows):
    wanted = first_block + jnp.arange(count_blocks, dtype=jnp.int32)
    chooser = (block_link[None, :] == wanted[:, None]).astype(jnp.float32)
    shaped = values.reshape(block_link.shape[0], block_rows, values.shape[1])
    placed = jnp.einsum("pi,ikn->pkn", chooser, shaped, precision=lax.Precision.HIGHEST)
    return placed.reshape(count_blocks * block_rows, values.shape[1])


def bit_pos_plus(bitpos):
    return bitpos + 1


def per_device(factor_inverse, contribution, block_map, sep_size, right_side):
    groups = lax.axis_size("sub")
    levels = groups.bit_length() - 1
    member = lax.axis_index("sub")
    position = lax.axis_index("front")
    row_count = right_side.shape[2]
    columns_rhs = right_side.shape[3]
    sep_rows = contribution.shape[2]
    block_count = block_map.shape[2]
    block_rows = sep_rows // block_count
    row_ids = position * row_count + jnp.arange(row_count, dtype=jnp.int32)
    keep_leaf = (row_ids < sep_size[0, 0])[:, None].astype(jnp.float32)
    keep_upper = (row_ids < sep_size[0, 1])[:, None].astype(jnp.float32)
    height = jnp.int32(levels + 1)
    for bitpos in range(levels):
        height = jnp.where(member % 2 ** bit_pos_plus(bitpos) == 2**bitpos, bitpos + 1, height)

    def solve(inverse, rhs_rows):
        return add_columns(
            inverse, lax.all_gather(rhs_rows.astype(jnp.bfloat16), "front", axis=0, tiled=True)
        )

    def descend(inverse, adjusted):
        source = adjusted.astype(jnp.bfloat16)
        return lax.psum_scatter(
            transpose_term(inverse, source), "front", scatter_dimension=0, tiled=True
        )

    def lift(update, source, block_link):
        product = jnp.dot(update, source.astype(jnp.bfloat16), preferred_element_type=jnp.float32)
        summed = lax.psum(product, "front")
        return place_blocks(
            block_link,
            summed,
            position * row_count // block_rows,
            row_count // block_rows,
            block_rows,
        )

    def rising_at(section):
        if section == 1:
            return member % 2 == 0
        if section - 1 < levels:
            return member >> section - 1 & 1 == 0
        return member < 0

    x_leaf = keep_leaf * solve(factor_inverse[0, 0], keep_leaf * right_side[0, 0])
    x_upper = jnp.zeros_like(x_leaf)
    for section in range(1, levels + 2):
        reach = 1 if section == 1 else 2 ** (section - 2)
        if section == 1:
            extended = lift(contribution[0, 0], x_leaf, block_map[0, 0])
            sending = member >= 0
        else:
            extended = lift(contribution[0, 1], x_upper, block_map[0, 1])
            sending = height == section - 1
        rising = rising_at(section)
        incoming = jnp.zeros_like(extended)
        if section <= levels:
            incoming = shifted(jnp.where(sending & rising, extended, 0.0), "sub", reach)
        if section == 1:
            incoming = incoming + jnp.where(rising, 0.0, extended)
        else:
            incoming = incoming + shifted(
                jnp.where(sending & jnp.logical_not(rising), extended, 0.0), "sub", -reach
            )
        candidate = keep_upper * solve(
            factor_inverse[0, 1], keep_upper * (right_side[0, 1] - incoming)
        )
        x_upper = jnp.where(height == section, candidate, x_upper)
    z_upper = jnp.where(
        height == levels + 1, keep_upper * descend(factor_inverse[0, 1], x_upper), 0.0
    )
    z_leaf = jnp.zeros_like(z_upper)
    chooser = (
        block_map[0, :, :, None] == jnp.arange(block_count, dtype=jnp.int32)[None, None, :]
    ).astype(jnp.bfloat16)
    for section in range(levels + 1, 0, -1):
        reach = 1 if section == 1 else 2 ** (section - 2)
        message = z_upper.astype(jnp.bfloat16)
        rising = rising_at(section)
        if section <= levels:
            from_above = shifted(message, "sub", -reach)
        else:
            from_above = message
        if section > 1:
            from_below = shifted(message, "sub", reach)
        else:
            from_below = message
        parent_slice = jnp.where(rising, from_above, from_below)
        gathered = lax.all_gather(parent_slice, "front", axis=0, tiled=True)
        slot = 0 if section == 1 else 1
        picked = jnp.einsum(
            "ip,pkn->ikn",
            chooser[slot],
            gathered.reshape(block_count, block_rows, columns_rhs),
            preferred_element_type=jnp.float32,
        )
        picked = picked.astype(jnp.bfloat16).reshape(sep_rows, columns_rhs)
        carried = jnp.einsum(
            "ir,in->rn", contribution[0, slot], picked, preferred_element_type=jnp.float32
        )
        if section == 1:
            adjusted = keep_leaf * (x_leaf - carried)
            z_leaf = keep_leaf * descend(factor_inverse[0, 0], adjusted)
        else:
            adjusted = keep_upper * (x_upper - carried)
            candidate = keep_upper * descend(factor_inverse[0, 1], adjusted)
            z_upper = jnp.where(height == section - 1, candidate, z_upper)
    return jnp.stack([z_leaf, z_upper])[None]


def solution(mesh):
    placed = (
        P("sub", None, "front", None),
        P("sub", None, None, "front"),
        P("sub", None, None),
        P("sub", None),
        P("sub", None, "front", None),
    )
    return jax.shard_map(
        per_device,
        mesh=mesh,
        in_specs=placed,
        out_specs=P("sub", None, "front", None),
        check_vma=False,
    )
```

profile of v0, /device:TPU:2, one launch (start us, length us, event | category | flops | bytes accessed | tf_op | source)
XLA Modules:
  0.0 998.8 jit_solution(5169525685779224775)
XLA Ops:
  10.5 40.9 %all-gather.8.cloned.1.call-done = bf16[4096,128]{0,1:T(8,128)(2,1)} async-done(((bf16[512,128]{0,1:T(8,128)(2,1)}), bf16[4096,128]{0,1:T(8,128)(2,1)}) %all-gather.8.cloned.1.call-update) | async-done | bytes 1048592 | tf_op jit(solution)/shard_map/all_gather | solution.py:52
  51.5 4.0 fusion.47
  55.5 3.7 fusion.38
  62.0 100.7 %all-reduce.4.cloned.1.call-done = f32[32,128,128]{2,0,1:T(8,128)} async-done(((f32[32,128,128]{2,0,1:T(8,128)}), f32[32,128,128]{2,0,1:T(8,128)}) %all-reduce.4.cloned.1.call-update) | async-done | bytes 2097168 | tf_op jit(solution)/shard_map/psum | solution.py:63
  168.1 4.8 collective-permute-done
  173.7 39.4 %all-gather.10.cloned.1.call-done = bf16[4096,128]{0,1:T(8,128)(2,1)} async-done(((bf16[512,128]{0,1:T(8,128)(2,1)}), bf16[4096,128]{0,1:T(8,128)(2,1)}) %all-gather.10.cloned.1.call-update) | async-done | bytes 1048592 | tf_op jit(solution)/shard_map/all_gather | solution.py:52
  213.1 4.0 fusion.92
  217.2 3.7 fusion.41
  223.6 100.7 %all-reduce.6.cloned.1.call-done = f32[32,128,128]{2,0,1:T(8,128)} async-done(((f32[32,128,128]{2,0,1:T(8,128)}), f32[32,128,128]{2,0,1:T(8,128)}) %all-reduce.6.cloned.1.call-update) | async-done | bytes 2097168 | tf_op jit(solution)/shard_map/psum | solution.py:63
  328.9 3.6 collective-permute-start.2
  337.4 39.7 %all-gather.12.cloned.1.call-done = bf16[4096,128]{0,1:T(8,128)(2,1)} async-done(((bf16[512,128]{0,1:T(8,128)(2,1)}), bf16[4096,128]{0,1:T(8,128)(2,1)}) %all-gather.12.cloned.1.call-update) | async-done | bytes 1048592 | tf_op jit(solution)/shard_map/all_gather | solution.py:52
  377.1 4.0 fusion.89
  381.2 3.7 fusion.44
  387.6 100.8 %all-reduce.8.cloned.1.call-done = f32[32,128,128]{2,0,1:T(8,128)} async-done(((f32[32,128,128]{2,0,1:T(8,128)}), f32[32,128,128]{2,0,1:T(8,128)}) %all-reduce.8.cloned.1.call-update) | async-done | bytes 2097168 | tf_op jit(solution)/shard_map/psum | solution.py:63
  490.9 2.5 collective-permute-start.3
  493.4 5.3 collective-permute-done.3
  499.4 40.7 %all-gather.14.cloned.1.call-done = bf16[4096,128]{0,1:T(8,128)(2,1)} async-done(((bf16[512,128]{0,1:T(8,128)(2,1)}), bf16[4096,128]{0,1:T(8,128)(2,1)}) %all-gather.14.cloned.1.call-update) | async-done | bytes 1048592 | tf_op jit(solution)/shard_map/all_gather | solution.py:52
  540.1 4.0 fusion.86
  544.2 4.3 convolution_bitcast_fusion.3
  548.5 67.0 %reduce-scatter.5.cloned.1.call-done = f32[512,128]{0,1:T(8,128)} async-done(((f32[4096,128]{0,1:T(8,128)}), f32[512,128]{0,1:T(8,128)}) %reduce-scatter.5.cloned.1.call-update) | async-done | bytes 262160 | tf_op jit(solution)/shard_map/reduce_scatter | solution.py:57
  617.9 5.6 collective-permute-done.4
  625.2 38.6 %all-gather.16.cloned.1.call-done = bf16[4096,128]{0,1:T(8,128)(2,1)} async-done(((bf16[512,128]{0,1:T(8,128)(2,1)}), bf16[4096,128]{0,1:T(8,128)(2,1)}) %all-gather.16.cloned.1.call-update) | async-done | bytes 1048592 | tf_op jit(solution)/shard_map/all_gather | solution.py:123
  667.7 6.3 convolution_bitcast_fusion.2
  674.1 67.3 %reduce-scatter.7.cloned.1.call-done = f32[512,128]{0,1:T(8,128)} async-done(((f32[4096,128]{0,1:T(8,128)}), f32[512,128]{0,1:T(8,128)}) %reduce-scatter.7.cloned.1.call-update) | async-done | bytes 262160 | tf_op jit(solution)/shard_map/reduce_scatter | solution.py:57
  746.8 3.8 collective-permute-done.6
  751.6 38.4 %all-gather.18.cloned.1.call-done = bf16[4096,128]{0,1:T(8,128)(2,1)} async-done(((bf16[512,128]{0,1:T(8,128)(2,1)}), bf16[4096,128]{0,1:T(8,128)(2,1)}) %all-gather.18.cloned.1.call-update) | async-done | bytes 1048592 | tf_op jit(solution)/shard_map/all_gather | solution.py:123
  793.9 6.3 convolution_bitcast_fusion.1
  800.2 67.3 %reduce-scatter.9.cloned.1.call-done = f32[512,128]{0,1:T(8,128)} async-done(((f32[4096,128]{0,1:T(8,128)}), f32[512,128]{0,1:T(8,128)}) %reduce-scatter.9.cloned.1.call-update) | async-done | bytes 262160 | tf_op jit(solution)/shard_map/reduce_scatter | solution.py:57
  870.4 2.5 collective-permute-done.7
  873.6 39.2 %all-gather.20.cloned.1.call-done = bf16[4096,128]{0,1:T(8,128)(2,1)} async-done(((bf16[512,128]{0,1:T(8,128)(2,1)}), bf16[4096,128]{0,1:T(8,128)(2,1)}) %all-gather.20.cloned.1.call-update) | async-done | bytes 1048592 | tf_op jit(solution)/shard_map/all_gather | solution.py:123
  916.6 6.3 convolution_bitcast_fusion
  923.0 67.3 %reduce-scatter.11.cloned.1.call-done = f32[512,128]{0,1:T(8,128)} async-done(((f32[4096,128]{0,1:T(8,128)}), f32[512,128]{0,1:T(8,128)}) %reduce-scatter.11.cloned.1.call-update) | async-done | bytes 262160 | tf_op jit(solution)/shard_map/reduce_scatter | solution.py:57
  (97 shorter events, 58.6 us)
Async XLA Ops:
  6.5 44.9 %all-gather.8.cloned.1.call-start = ((), (), s32[]{:S(2)}) async-start(), calls=%async_computation.4 | async-start | bytes 1179648 | tf_op jit(solution)/shard_map/all_gather | solution.py:52
  10.5 152.2 %all-reduce.4.cloned.1.call-start = ((), (), s32[]{:S(2)}) async-start(), calls=%async_computation.5 | async-start | bytes 4194304 | tf_op jit(solution)/shard_map/psum | solution.py:63
  59.5 2.4 copy-start.2
  61.9 151.3 %all-gather.10.cloned.1.call-start = ((), (), s32[]{:S(2)}) async-start(), calls=%async_computation.6 | async-start | bytes 1179648 | tf_op jit(solution)/shard_map/all_gather | solution.py:52
  165.2 7.7 collective-permute-start
  173.6 150.6 %all-reduce.6.cloned.1.call-start = ((), (), s32[]{:S(2)}) async-start(), calls=%async_computation.7 | async-start | bytes 4194304 | tf_op jit(solution)/shard_map/psum | solution.py:63
  223.5 153.6 %all-gather.12.cloned.1.call-start = ((), (), s32[]{:S(2)}) async-start(), calls=%async_computation.8 | async-start | bytes 1179648 | tf_op jit(solution)/shard_map/all_gather | solution.py:52
  326.8 7.7 collective-permute-start.1
  328.9 7.5 collective-permute-start.2
  337.2 151.2 %all-reduce.8.cloned.1.call-start = ((), (), s32[]{:S(2)}) async-start(), calls=%async_computation.9 | async-start | bytes 4194304 | tf_op jit(solution)/shard_map/psum | solution.py:63
  387.5 152.6 %all-gather.14.cloned.1.call-start = ((), (), s32[]{:S(2)}) async-start(), calls=%async_computation.10 | async-start | bytes 1179648 | tf_op jit(solution)/shard_map/all_gather | solution.py:52
  490.9 7.8 collective-permute-start.3
  499.4 116.2 %reduce-scatter.5.cloned.1.call-start = ((), (), s32[]{:S(2)}) async-start(), calls=%async_computation.11 | async-start | bytes 2359296 | tf_op jit(solution)/shard_map/reduce_scatter | solution.py:57
  548.5 115.4 %all-gather.16.cloned.1.call-start = ((), (), s32[]{:S(2)}) async-start(), calls=%async_computation.12 | async-start | bytes 1179648 | tf_op jit(solution)/shard_map/all_gather | solution.py:123
  616.6 6.9 collective-permute-start.4
  625.1 116.3 %reduce-scatter.7.cloned.1.call-start = ((), (), s32[]{:S(2)}) async-start(), calls=%async_computation.13 | async-start | bytes 2359296 | tf_op jit(solution)/shard_map/reduce_scatter | solution.py:57
  667.7 73.7 %copy-start = (f32[512,128]{0,1:T(8,128)S(1)}, f32[512,128]{0,1:T(8,128)}, u32[]{:S(2)}) copy-start(f32[512,128]{0,1:T(8,128)} %reduce-scatter.5.cloned.1.call-done) | copy-start | bytes 786436
  674.0 116.0 %all-gather.18.cloned.1.call-start = ((), (), s32[]{:S(2)}) async-start(), calls=%async_computation.14 | async-start | bytes 1179648 | tf_op jit(solution)/shard_map/all_gather | solution.py:123
  742.4 4.4 collective-permute-start.5
  744.3 6.3 collective-permute-start.6
  751.3 116.1 %reduce-scatter.9.cloned.1.call-start = ((), (), s32[]{:S(2)}) async-start(), calls=%async_computation.15 | async-start | bytes 2359296 | tf_op jit(solution)/shard_map/reduce_scatter | solution.py:57
  800.2 112.6 %all-gather.20.cloned.1.call-start = ((), (), s32[]{:S(2)}) async-start(), calls=%async_computation.16 | async-start | bytes 1179648 | tf_op jit(solution)/shard_map/all_gather | solution.py:123
  868.5 4.4 collective-permute-start.7
  873.6 116.7 %reduce-scatter.11.cloned.1.call-start = ((), (), s32[]{:S(2)}) async-start(), calls=%async_computation.17 | async-start | bytes 2359296 | tf_op jit(solution)/shard_map/reduce_scatter | solution.py:57
  916.6 6.3 copy-start.1
Sparse Core Ops, SparseCore 0:
  10.6 40.8 all-gather.7
  62.0 100.6 all-reduce.3
  173.8 39.3 all-gather.9
  223.6 100.5 all-reduce.5
  337.3 39.7 all-gather.11
  387.6 100.6 all-reduce.7
  499.5 40.6 all-gather.13
  548.6 66.9 reduce-scatter.4
  625.2 38.5 all-gather.15
  674.1 67.2 reduce-scatter.6
  751.4 38.5 all-gather.17
  800.3 67.1 reduce-scatter.8
  873.7 39.0 all-gather.19
  923.0 67.1 reduce-scatter.10
where the time goes:
time: 1000 us; the launch traced here: 999 us
  waiting for transfers between devices  874 us (87%)
  matrix products  58.6 us (6%)
  local copies, waits for them, and re-layouts  22.5 us (2%)
  starting transfers between devices  18.4 us (2%)
  between operations  13.8 us (1%)
  other arithmetic  11.2 us (1%)
    psum x3, waiting for transfers between devices, lift(): summed = lax.psum(product, 'front')  302 us
    reduce_scatter x4, waiting for transfers between devices, descend(): lax.psum_scatter(transpose_term(inverse, source), 'front', scatter_dimens...  269 us
    all_gather x4, waiting for transfers between devices, solve(): lax.all_gather(rhs_rows.astype(jnp.bfloat16), 'front', axis=0, tiled=True)  161 us
    all_gather x3, waiting for transfers between devices, per_device(): gathered = lax.all_gather(parent_slice, 'front', axis=0, tiled=True)  116 us
    ppermute x8, waiting for transfers between devices, shifted(): lax.ppermute(value, axis, [(source, source + steps) for source in range(f...  25.9 us
    dot_general x4, matrix products, transpose_term(): jnp.einsum('rc,rn->cn', inverse, source, preferred_element_type=jnp.float32)  23.1 us
  transfers between devices with their start and end apart: 22, of which 22 were waited for; matrix products, arithmetic and copies ran while one was open for 0% of the time, Pallas kernels for 0%

commit v1 on v0

v1 whole, which is shorter than its diff:
```python
import functools

import jax
import jax.numpy as jnp
from jax import lax
from jax.experimental import pallas as pl
from jax.experimental.pallas import tpu as pltpu
from jax.sharding import PartitionSpec as P

MESH = pl.DeviceIdType.MESH
F32 = jnp.float32
BF16 = jnp.bfloat16


def tree(groups):
    levels = groups.bit_length() - 1
    heights, parents = [], []
    for g in range(groups):
        height = levels + 1
        if g:
            height = 1
            while (g >> (height - 1)) & 1 == 0:
                height += 1
        heights.append(height)
        if height == levels + 1:
            parents.append(0)
        elif height == levels:
            parents.append(0)
        else:
            reach = 2 ** (height - 1)
            parents.append(g + reach if (g >> height) & 1 == 0 else g - reach)
    first, second, slots = [], [], []
    for g in range(groups):
        kids = [c for c in range(1, groups) if parents[c] == g]
        first.append(kids[0] if kids else 0)
        second.append(kids[1] if len(kids) > 1 else -1)
        slots.append(0 if g == 0 else [c for c in range(1, groups) if parents[c] == parents[g]].index(g))
    return heights, parents, first, second, slots


def pick(table, index):
    value = jnp.int32(table[0])
    for position in range(1, len(table)):
        value = jnp.where(index == position, jnp.int32(table[position]), value)
    return value


def remote(src, dst, send, recv, device):
    return pltpu.make_async_remote_copy(
        src_ref=src, dst_ref=dst, send_sem=send, recv_sem=recv, device_id=device, device_id_type=MESH
    )


def loop(low, high, body):
    def step(index, carry):
        body(index)
        return carry

    lax.fori_loop(low, high, step, 0)


def kernel(
    groups, hi, lo,
    sep, inv, rhs, li_hbm, co_hbm, out,
    li, co0, co1, ag, agb, st, stb, p1, p1b, p2, p2b, cross, xb, ab, zs, acc, xs, acct,
    wsem, s_ag1, s_ag2, r_ag, s_1, r_1, s_2, r_2, s_x, r_x,
    s_b1, r_b1, s_b2, r_b2, s_par, s_gb1, s_gb2, r_gb, s_xb,
):
    heights, parents, first, second, slots = tree(groups)
    m = lax.axis_index("sub")
    f = lax.axis_index("front")
    h, l = f // lo, f % lo
    rows, n = rhs.shape[1], rhs.shape[2]
    co = (co0, co1)
    per = co0.shape[0] // (hi * lo)
    parent, slot = pick(parents, m), pick(slots, m)
    kid0, kid1 = pick(first, m), pick(second, m)
    top = m == 0
    odd = m % 2 == 1
    two = kid1 >= 0
    mate = jnp.where(odd, m - 1, m + 1)

    weights = [
        pltpu.make_async_copy(li_hbm.at[0], li.at[0], wsem.at[0]),
        pltpu.make_async_copy(co_hbm.at[0], co0, wsem.at[1]),
        pltpu.make_async_copy(li_hbm.at[1], li.at[1], wsem.at[2]),
        pltpu.make_async_copy(co_hbm.at[1], co1, wsem.at[3]),
    ]
    for weight in weights:
        weight.start()

    barrier = pltpu.get_barrier_semaphore()
    count = 0
    for d in range(1, hi):
        pl.semaphore_signal(barrier, inc=1, device_id=(m, (h + d) % hi * lo + l), device_id_type=MESH)
        count += 1
    for e in range(1, lo):
        pl.semaphore_signal(barrier, inc=1, device_id=(m, h * lo + (l + e) % lo), device_id_type=MESH)
        count += 1
    for g in range(1, groups):
        for d in range(hi):
            pl.semaphore_signal(
                barrier, inc=1, device_id=((m + g) % groups, (h + d) % hi * lo + l), device_id_type=MESH
            )
            count += 1

    def keep_rows(k):
        return f * rows + lax.broadcasted_iota(jnp.int32, (rows, n), 0) < sep[0, k]

    def keep_columns(k):
        return f * rows + lax.broadcasted_iota(jnp.int32, (n, rows), 1) < sep[0, k]

    def away(d):
        return (h + hi - d) % hi

    def peer(e):
        return h * lo + (l + e) % lo

    def blocks(k, q):
        return jnp.concatenate([co[k][inv[k, q * per + j]] for j in range(per)], axis=0)

    def columns(k, q):
        return li[k, :, pl.ds(pl.multiple_of(q * rows, rows), rows)]

    def ag_hi(k, d):
        return remote(ag.at[k, f], ag.at[k, f], s_ag1.at[k, d], r_ag.at[k, f], (m, (h + d) % hi * lo + l))

    def ag_lo(k, q, e, d):
        return remote(ag.at[k, q], ag.at[k, q], s_ag2.at[k, e, d], r_ag.at[k, q], (m, peer(e)))

    def gather(k, consume):
        for d in range(1, hi):
            ag_hi(k, d).start()
        for e in range(1, lo):
            ag_lo(k, f, e, 0).start()
        consume(f)

        def from_hi(d):
            q = away(d) * lo + l
            ag_lo(k, q, 0, 0).wait_recv()
            for e in range(1, lo):
                ag_lo(k, q, e, d).start()
            consume(q)

        loop(1, hi, from_hi)
        for e in range(1, lo):
            def from_lo(d):
                q = away(d) * lo + (l + lo - e) % lo
                ag_lo(k, q, 0, 0).wait_recv()
                consume(q)

            loop(0, hi, from_lo)

    def gather_sent(k):
        for d in range(1, hi):
            ag_hi(k, d).wait_send()
        for e in range(1, lo):
            loop(0, hi, lambda d: ag_lo(k, away(d) * lo + l, e, d).wait_send())

    def rs1(st_, p_, s_, r_, k, e, h2):
        q = h2 * lo + (l + e) % lo
        return remote(st_.at[k, q], p_.at[k, e, h2], s_.at[k, e, h2], r_.at[k, e, h2], (m, peer(e)))

    def reduce_lo(bufs, k, produce, finish, steps):
        st_, p_, s_, r_ = bufs
        for e in range(1, lo):
            def send(d):
                h2 = (h + 1 + d) % hi
                q = h2 * lo + (l + e) % lo
                st_[k, q] = produce(q).astype(BF16)
                rs1(st_, p_, s_, r_, k, e, h2).start()

            loop(0, hi, send)

        def total(h2):
            value = produce(h2 * lo + l)
            for e in range(1, lo):
                rs1(st_, p_, s_, r_, k, e, h2).wait_recv()
                value = value + p_[k, e, h2].astype(F32)
            return value.astype(BF16)

        def body(d):
            h2 = (h + 1 + d) % hi
            st_[k, h2 * lo + l] = total(h2)
            finish(h2)

        loop(0, steps, body)
        return total

    def reduce_sent(bufs, k):
        st_, p_, s_, r_ = bufs
        for e in range(1, lo):
            loop(0, hi, lambda h2: rs1(st_, p_, s_, r_, k, e, h2).wait_send())

    up = (st, p1, s_1, r_1)
    down = (stb, p1b, s_b1, r_b1)

    def rs2(k, c, dst, h2):
        return remote(st.at[k, h2 * lo + l], p2.at[c, h], s_2.at[k, h2], r_2.at[c, h], (dst, h2 * lo + l))

    def wait2(c, h2):
        remote(p2.at[c, h2], p2.at[c, h2], s_2.at[0, 0], r_2.at[c, h2], (mate, f)).wait_recv()

    def rs2b(k, h2):
        return remote(stb.at[k, h2 * lo + l], p2b.at[k, h], s_b2.at[k, h2], r_b2.at[k, h], (m, h2 * lo + l))

    def to_mate(q):
        return remote(st.at[0, q], cross.at[q], s_x.at[q], r_x.at[q], (mate, f))

    def solve(k):
        acc[...] = jnp.zeros_like(acc)

        def consume(q):
            acc[...] += jnp.dot(columns(k, q), ag[k, q], preferred_element_type=F32)

        return consume

    ag[0, f] = jnp.where(keep_rows(0), rhs[0], 0.0).astype(BF16)
    pl.semaphore_wait(barrier, count)
    weights[0].wait()
    gather(0, solve(0))
    leaf = jnp.where(keep_rows(0), acc[...], 0.0)
    xs[0] = leaf.T
    xb[...] = leaf.astype(BF16)
    weights[1].wait()

    def lifted(k):
        return lambda q: jnp.dot(blocks(k, q), xb[...], preferred_element_type=F32)

    @pl.when(jnp.logical_not(odd))
    def _():
        for e in list(range(1, lo)) + [0]:
            def send(d):
                q = (h + 1 + d) % hi * lo + (l + e) % lo
                st[0, q] = lifted(0)(q).astype(BF16)
                to_mate(q).start()

            loop(0, hi, send)

    @pl.when(odd)
    def _():
        def produce(q):
            value = lifted(0)(q)
            to_mate(q).wait_recv()
            return value + cross[q].astype(F32)

        total = reduce_lo(up, 0, produce, lambda h2: rs2(0, 0, m, h2).start(), hi - 1)
        p2[0, h] = total(h)
        loop(1, hi, lambda d: wait2(0, away(d)))

    @pl.when(jnp.logical_not(odd))
    def _():
        loop(0, hi, lambda h2: wait2(0, h2))

    incoming = p2[0, 0].astype(F32)
    for h2 in range(1, hi):
        incoming = incoming + p2[0, h2].astype(F32)
    acc[...] = rhs[1] - incoming

    @pl.when(two)
    def _():
        loop(0, hi, lambda h2: wait2(1, h2))
        other = p2[1, 0].astype(F32)
        for h2 in range(1, hi):
            other = other + p2[1, h2].astype(F32)
        acc[...] -= other

    ag[1, f] = jnp.where(keep_rows(1), acc[...], 0.0).astype(BF16)
    weights[2].wait()
    gather(1, solve(1))
    upper = jnp.where(keep_rows(1), acc[...], 0.0)
    xs[1] = upper.T
    xb[...] = upper.astype(BF16)
    weights[3].wait()

    def to_child(c, kid, h2):
        return remote(zs, agb.at[1, f], s_par.at[c, h2], r_gb.at[1, f], (kid, h2 * lo + l))

    def gb_lo(k, q, e, d):
        return remote(agb.at[k, q], agb.at[k, q], s_gb2.at[k, e, d], r_gb.at[k, q], (m, peer(e)))

    def gb_hi(d):
        return remote(agb.at[0, f], agb.at[0, f], s_gb1.at[d], r_gb.at[0, f], (m, (h + d) % hi * lo + l))

    def gb_mate(q):
        return remote(agb.at[0, q], agb.at[0, q], s_xb.at[q], r_gb.at[0, q], (mate, f))

    def carry(k, q):
        acct[...] += jnp.dot(agb[k, q], blocks(k, q), preferred_element_type=F32)

    acct[...] = jnp.zeros_like(acct)

    @pl.when(jnp.logical_not(top))
    def _():
        reduce_lo(up, 1, lifted(1), lambda h2: rs2(1, slot, parent, h2).start(), hi)

        def from_parent(d):
            q = away(d) * lo + l
            gb_lo(1, q, 0, 0).wait_recv()
            for e in range(1, lo):
                gb_lo(1, q, e, d).start()
            carry(1, q)

        loop(0, hi, from_parent)
        for e in range(1, lo):
            def from_lo(d):
                q = away(d) * lo + (l + lo - e) % lo
                gb_lo(1, q, 0, 0).wait_recv()
                carry(1, q)

            loop(0, hi, from_lo)

    def descend(k):
        ab[...] = jnp.where(keep_columns(k), xs[k] - acct[...], 0.0).astype(BF16)

        def produce(q):
            return jnp.dot(ab[...], columns(k, q), preferred_element_type=F32)

        total = reduce_lo(down, k, produce, lambda h2: rs2b(k, h2).start(), hi - 1)
        value = total(h).astype(F32)

        def collect(d):
            source = away(d)
            remote(
                p2b.at[k, source], p2b.at[k, source], s_b2.at[k, 0], r_b2.at[k, source], (mate, f)
            ).wait_recv()
            return p2b[k, source].astype(F32)

        for d in range(1, hi):
            value = value + collect(d)
        return jnp.where(keep_columns(k), value, 0.0)

    solved = descend(1)
    zs[...] = solved.astype(BF16)

    @pl.when(jnp.logical_not(odd))
    def _():
        loop(0, hi, lambda d: to_child(0, kid0, (h + d) % hi).start())

    @pl.when(two)
    def _():
        loop(0, hi, lambda d: to_child(1, kid1, (h + d) % hi).start())

    acct[...] = jnp.zeros_like(acct)

    @pl.when(odd)
    def _():
        agb[0, f] = zs[...]
        for d in range(1, hi):
            gb_hi(d).start()
        for e in range(1, lo):
            gb_lo(0, f, e, 0).start()
        gb_mate(f).start()
        carry(0, f)

        def from_hi(d):
            q = away(d) * lo + l
            gb_lo(0, q, 0, 0).wait_recv()
            for e in range(1, lo):
                gb_lo(0, q, e, d).start()
            gb_mate(q).start()
            carry(0, q)

        loop(1, hi, from_hi)
        for e in range(1, lo):
            def from_lo(d):
                q = away(d) * lo + (l + lo - e) % lo
                gb_lo(0, q, 0, 0).wait_recv()
                gb_mate(q).start()
                carry(0, q)

            loop(0, hi, from_lo)

    out[1] = solved.T

    @pl.when(jnp.logical_not(odd))
    def _():
        for e in range(lo):
            def from_mate(d):
                q = away(d) * lo + (l + lo - e) % lo
                gb_lo(0, q, 0, 0).wait_recv()
                carry(0, q)

            loop(0, hi, from_mate)

    out[0] = descend(0).T

    for k in range(2):
        gather_sent(k)
        reduce_sent(down, k)
        loop(1, hi, lambda d: rs2b(k, (h + d) % hi).wait_send())

    @pl.when(jnp.logical_not(top))
    def _():
        reduce_sent(up, 1)
        loop(0, hi, lambda h2: rs2(1, slot, parent, h2).wait_send())
        for e in range(1, lo):
            loop(0, hi, lambda d: gb_lo(1, away(d) * lo + l, e, d).wait_send())

    @pl.when(jnp.logical_not(odd))
    def _():
        loop(0, hi * lo, lambda q: to_mate(q).wait_send())
        loop(0, hi, lambda d: to_child(0, kid0, (h + d) % hi).wait_send())

    @pl.when(two)
    def _():
        loop(0, hi, lambda d: to_child(1, kid1, (h + d) % hi).wait_send())

    @pl.when(odd)
    def _():
        reduce_sent(up, 0)
        loop(1, hi, lambda d: rs2(0, 0, m, (h + d) % hi).wait_send())
        for d in range(1, hi):
            gb_hi(d).wait_send()
        for e in range(1, lo):
            loop(0, hi, lambda d: gb_lo(0, away(d) * lo + l, e, d).wait_send())
        loop(0, hi * lo, lambda q: gb_mate(q).wait_send())


def per_device(hi, lo, factor_inverse, contribution, block_map, sep_size, right_side):
    groups = lax.axis_size("sub")
    rows, n = right_side.shape[2:]
    sep_rows = contribution.shape[2]
    count = block_map.shape[2]
    fronts = hi * lo
    steps = jnp.arange(count, dtype=jnp.int32)
    inverse = jnp.sum(
        jnp.where(block_map[0][:, :, None] == steps[None, None, :], steps[None, :, None], 0), axis=1
    )
    dma = pltpu.SemaphoreType.DMA
    vmem = pl.BlockSpec(memory_space=pltpu.VMEM)
    smem = pl.BlockSpec(memory_space=pltpu.SMEM)
    hbm = pl.BlockSpec(memory_space=pl.ANY)
    out = pl.pallas_call(
        functools.partial(kernel, groups, hi, lo),
        out_shape=jax.ShapeDtypeStruct((2, rows, n), F32),
        in_specs=[smem, smem, vmem, hbm, hbm],
        out_specs=vmem,
        scratch_shapes=[
            pltpu.VMEM((2, rows, sep_rows), BF16),
            pltpu.VMEM((count, sep_rows // count, rows), BF16),
            pltpu.VMEM((count, sep_rows // count, rows), BF16),
            pltpu.VMEM((2, fronts, rows, n), BF16),
            pltpu.VMEM((2, fronts, n, rows), BF16),
            pltpu.VMEM((2, fronts, rows, n), BF16),
            pltpu.VMEM((2, fronts, n, rows), BF16),
            pltpu.VMEM((2, lo, hi, rows, n), BF16),
            pltpu.VMEM((2, lo, hi, n, rows), BF16),
            pltpu.VMEM((2, hi, rows, n), BF16),
            pltpu.VMEM((2, hi, n, rows), BF16),
            pltpu.VMEM((fronts, rows, n), BF16),
            pltpu.VMEM((rows, n), BF16),
            pltpu.VMEM((n, rows), BF16),
            pltpu.VMEM((n, rows), BF16),
            pltpu.VMEM((rows, n), F32),
            pltpu.VMEM((2, n, rows), F32),
            pltpu.VMEM((n, rows), F32),
            dma((4,)),
            dma((2, hi)), dma((2, lo, hi)), dma((2, fronts)),
            dma((2, lo, hi)), dma((2, lo, hi)),
            dma((2, hi)), dma((2, hi)),
            dma((fronts,)), dma((fronts,)),
            dma((2, lo, hi)), dma((2, lo, hi)),
            dma((2, hi)), dma((2, hi)),
            dma((2, hi)), dma((hi,)), dma((2, lo, hi)), dma((2, fronts)), dma((fronts,)),
        ],
        compiler_params=pltpu.CompilerParams(
            collective_id=0, has_side_effects=True, vmem_limit_bytes=56 * 1024 * 1024
        ),
    )(
        sep_size,
        inverse,
        right_side[0],
        factor_inverse[0],
        contribution[0].reshape(2, count, sep_rows // count, rows),
    )
    return out[None]


def solution(mesh):
    fronts = mesh.shape["front"]
    hi = min(4, fronts)
    placed = (
        P("sub", None, "front", None),
        P("sub", None, None, "front"),
        P("sub", None, None),
        P("sub", None),
        P("sub", None, "front", None),
    )
    return jax.shard_map(
        functools.partial(per_device, hi, fronts // hi),
        mesh=mesh,
        in_specs=placed,
        out_specs=P("sub", None, "front", None),
        check_vma=False,
    )
```

time: 1000 us -> 213 us (0.21)
  waiting for transfers between devices: 874 us -> 0 us
  Pallas kernels: 0 us -> 207 us
  matrix products: 58.6 us -> 0 us
  local copies, waits for them, and re-layouts: 22.5 us -> 1.87 us
  starting transfers between devices: 18.4 us -> 0 us
  between operations: 13.8 us -> 0.01 us
    psum x3 -> x0, waiting for transfers between devices: 302 us -> none  [lift(): summed = lax.psum(product, 'front')]
    all_gather x7 -> x0, waiting for transfers between devices: 277 us -> none  [the longest x4 161 us: solve(): lax.all_gather(rhs_rows.astype(jnp.bfloat16), 'front', axis=0, tiled=True)]
    reduce_scatter x4 -> x0, waiting for transfers between devices: 269 us -> none  [descend(): lax.psum_scatter(transpose_term(inverse, source), 'front', scatter_dimens...]
    pallas_call x0 -> x1, Pallas kernels: none -> 207 us  [per_device(): pl.pallas_call(functools.partial(kernel, groups, hi, lo), out_shape=jax.S...]
    dot_general x17 -> x0, matrix products: 58.6 us -> none  [the longest x4 23.1 us: transpose_term(): jnp.einsum('rc,rn->cn', inverse, source, preferred_element_type=jnp.float32)]
    ppermute x8 -> x0, waiting for transfers between devices: 25.9 us -> none  [shifted(): lax.ppermute(value, axis, [(source, source + steps) for source in range(f...]
    ppermute x8 -> x0, starting transfers between devices: 17.5 us -> none  [shifted(): lax.ppermute(value, axis, [(source, source + steps) for source in range(f...]
    reshape x6 -> x0, local copies, waits for them, and re-layouts: 11.4 us -> none  [the longest x3 6.82 us: place_blocks(): shaped = values.reshape(block_link.shape[0], block_rows, values.shape[1])]
  transfers between devices with their start and end apart: 22 -> 0, of which waited for: 22 -> 0; matrix products, arithmetic and copies ran while one was open for 0% -> 0% of each run, Pallas kernels for 0% -> 0%
where the time goes in v1:
time: 213 us; the launch traced here: 210 us
  Pallas kernels  207 us (97%)
    pallas_call x1, Pallas kernels, per_device(): pl.pallas_call(functools.partial(kernel, groups, hi, lo), out_shape=jax.S...  207 us

profile of v1, /device:TPU:2, one launch (start us, length us, event | category | flops | bytes accessed | tf_op | source)
XLA Modules:
  0.0 210.5 jit_solution(10913110839814131569)
XLA Ops:
  0.0 1.3 select_reduce_fusion.inv
  1.3 207.3 %shard_map.55 = f32[2,512,128]{2,1,0:T(8,128)} custom-call(s32[1,2]{1,0:T(1,128)} %sep.1, s32[2,32]{1,0:T(2,128)} %select_reduce_fusion.inv, f32[2,512,128]{2,1,0:T(8,128)} %bitcast.8, bf16[2,512,4096]{2,1,0:T(8,128)(2,1)} %bitcast.5, bf16[2,32,128,512]{3,2,1,0:T(8,128)(2,1)} %bitcast.6), custom_call_target="tpu_custom_call" | custom-call | tf_op jit(solution)/shard_map/pallas_call | solution.py:434
  208.6 1.9 copy.7

commit v2 on v1

--- a/solution.py
+++ b/solution.py
@@ -39,9 +39,9 @@
 
 
 def pick(table, index):
-    value = jnp.int32(table[0])
+    value = table[0] + jnp.int32(0)
     for position in range(1, len(table)):
-        value = jnp.where(index == position, jnp.int32(table[position]), value)
+        value = jnp.where(index == position, table[position] + jnp.int32(0), value)
     return value
 
 
@@ -110,8 +110,13 @@
     def keep_columns(k):
         return f * rows + lax.broadcasted_iota(jnp.int32, (n, rows), 1) < sep[0, k]
 
-    def away(d):
-        return (h + hi - d) % hi
+    order = [sorted(range(hi), key=lambda other: (abs(other - own), other)) for own in range(hi)]
+    nearest = [pick([order[own][d] for own in range(hi)], h) for d in range(hi)]
+
+    def near(d):
+        if isinstance(d, int):
+            return nearest[d]
+        return pick(nearest, d)
 
     def peer(e):
         return h * lo + (l + e) % lo
@@ -123,7 +128,7 @@
         return li[k, :, pl.ds(pl.multiple_of(q * rows, rows), rows)]
 
     def ag_hi(k, d):
-        return remote(ag.at[k, f], ag.at[k, f], s_ag1.at[k, d], r_ag.at[k, f], (m, (h + d) % hi * lo + l))
+        return remote(ag.at[k, f], ag.at[k, f], s_ag1.at[k, d], r_ag.at[k, f], (m, near(d) * lo + l))
 
     def ag_lo(k, q, e, d):
         return remote(ag.at[k, q], ag.at[k, q], s_ag2.at[k, e, d], r_ag.at[k, q], (m, peer(e)))
@@ -136,7 +141,7 @@
         consume(f)
 
         def from_hi(d):
-            q = away(d) * lo + l
+            q = near(d) * lo + l
             ag_lo(k, q, 0, 0).wait_recv()
             for e in range(1, lo):
                 ag_lo(k, q, e, d).start()
@@ -145,7 +150,7 @@
         loop(1, hi, from_hi)
         for e in range(1, lo):
             def from_lo(d):
-                q = away(d) * lo + (l + lo - e) % lo
+                q = near(d) * lo + (l + lo - e) % lo
                 ag_lo(k, q, 0, 0).wait_recv()
                 consume(q)
 
@@ -155,7 +160,7 @@
         for d in range(1, hi):
             ag_hi(k, d).wait_send()
         for e in range(1, lo):
-            loop(0, hi, lambda d: ag_lo(k, away(d) * lo + l, e, d).wait_send())
+            loop(0, hi, lambda d: ag_lo(k, near(d) * lo + l, e, d).wait_send())
 
     def rs1(st_, p_, s_, r_, k, e, h2):
         q = h2 * lo + (l + e) % lo
@@ -165,7 +170,7 @@
         st_, p_, s_, r_ = bufs
         for e in range(1, lo):
             def send(d):
-                h2 = (h + 1 + d) % hi
+                h2 = near((d + 1) % hi)
                 q = h2 * lo + (l + e) % lo
                 st_[k, q] = produce(q).astype(BF16)
                 rs1(st_, p_, s_, r_, k, e, h2).start()
@@ -180,7 +185,7 @@
             return value.astype(BF16)
 
         def body(d):
-            h2 = (h + 1 + d) % hi
+            h2 = near((d + 1) % hi)
             st_[k, h2 * lo + l] = total(h2)
             finish(h2)
 
@@ -231,7 +236,7 @@
     def _():
         for e in list(range(1, lo)) + [0]:
             def send(d):
-                q = (h + 1 + d) % hi * lo + (l + e) % lo
+                q = near((d + 1) % hi) * lo + (l + e) % lo
                 st[0, q] = lifted(0)(q).astype(BF16)
                 to_mate(q).start()
 
@@ -246,7 +251,7 @@
 
         total = reduce_lo(up, 0, produce, lambda h2: rs2(0, 0, m, h2).start(), hi - 1)
         p2[0, h] = total(h)
-        loop(1, hi, lambda d: wait2(0, away(d)))
+        loop(1, hi, lambda d: wait2(0, near(d)))
 
     @pl.when(jnp.logical_not(odd))
     def _():
@@ -280,7 +285,7 @@
         return remote(agb.at[k, q], agb.at[k, q], s_gb2.at[k, e, d], r_gb.at[k, q], (m, peer(e)))
 
     def gb_hi(d):
-        return remote(agb.at[0, f], agb.at[0, f], s_gb1.at[d], r_gb.at[0, f], (m, (h + d) % hi * lo + l))
+        return remote(agb.at[0, f], agb.at[0, f], s_gb1.at[d], r_gb.at[0, f], (m, near(d) * lo + l))
 
     def gb_mate(q):
         return remote(agb.at[0, q], agb.at[0, q], s_xb.at[q], r_gb.at[0, q], (mate, f))
@@ -295,7 +300,7 @@
         reduce_lo(up, 1, lifted(1), lambda h2: rs2(1, slot, parent, h2).start(), hi)
 
         def from_parent(d):
-            q = away(d) * lo + l
+            q = near(d) * lo + l
             gb_lo(1, q, 0, 0).wait_recv()
             for e in range(1, lo):
                 gb_lo(1, q, e, d).start()
@@ -304,7 +309,7 @@
         loop(0, hi, from_parent)
         for e in range(1, lo):
             def from_lo(d):
-                q = away(d) * lo + (l + lo - e) % lo
+                q = near(d) * lo + (l + lo - e) % lo
                 gb_lo(1, q, 0, 0).wait_recv()
                 carry(1, q)
 
@@ -320,7 +325,7 @@
         value = total(h).astype(F32)
 
         def collect(d):
-            source = away(d)
+            source = near(d)
             remote(
                 p2b.at[k, source], p2b.at[k, source], s_b2.at[k, 0], r_b2.at[k, source], (mate, f)
             ).wait_recv()
@@ -335,11 +340,11 @@
 
     @pl.when(jnp.logical_not(odd))
     def _():
-        loop(0, hi, lambda d: to_child(0, kid0, (h + d) % hi).start())
+        loop(0, hi, lambda d: to_child(0, kid0, near(d)).start())
 
     @pl.when(two)
     def _():
-        loop(0, hi, lambda d: to_child(1, kid1, (h + d) % hi).start())
+        loop(0, hi, lambda d: to_child(1, kid1, near(d)).start())
 
     acct[...] = jnp.zeros_like(acct)
 
@@ -354,7 +359,7 @@
         carry(0, f)
 
         def from_hi(d):
-            q = away(d) * lo + l
+            q = near(d) * lo + l
             gb_lo(0, q, 0, 0).wait_recv()
             for e in range(1, lo):
                 gb_lo(0, q, e, d).start()
@@ -364,7 +369,7 @@
         loop(1, hi, from_hi)
         for e in range(1, lo):
             def from_lo(d):
-                q = away(d) * lo + (l + lo - e) % lo
+                q = near(d) * lo + (l + lo - e) % lo
                 gb_lo(0, q, 0, 0).wait_recv()
                 gb_mate(q).start()
                 carry(0, q)
@@ -377,7 +382,7 @@
     def _():
         for e in range(lo):
             def from_mate(d):
-                q = away(d) * lo + (l + lo - e) % lo
+                q = near(d) * lo + (l + lo - e) % lo
                 gb_lo(0, q, 0, 0).wait_recv()
                 carry(0, q)
 
@@ -395,16 +400,16 @@
         reduce_sent(up, 1)
         loop(0, hi, lambda h2: rs2(1, slot, parent, h2).wait_send())
         for e in range(1, lo):
-            loop(0, hi, lambda d: gb_lo(1, away(d) * lo + l, e, d).wait_send())
+            loop(0, hi, lambda d: gb_lo(1, near(d) * lo + l, e, d).wait_send())
 
     @pl.when(jnp.logical_not(odd))
     def _():
         loop(0, hi * lo, lambda q: to_mate(q).wait_send())
-        loop(0, hi, lambda d: to_child(0, kid0, (h + d) % hi).wait_send())
+        loop(0, hi, lambda d: to_child(0, kid0, near(d)).wait_send())
 
     @pl.when(two)
     def _():
-        loop(0, hi, lambda d: to_child(1, kid1, (h + d) % hi).wait_send())
+        loop(0, hi, lambda d: to_child(1, kid1, near(d)).wait_send())
 
     @pl.when(odd)
     def _():
@@ -413,7 +418,7 @@
         for d in range(1, hi):
             gb_hi(d).wait_send()
         for e in range(1, lo):
-            loop(0, hi, lambda d: gb_lo(0, away(d) * lo + l, e, d).wait_send())
+            loop(0, hi, lambda d: gb_lo(0, near(d) * lo + l, e, d).wait_send())
         loop(0, hi * lo, lambda q: gb_mate(q).wait_send())
 
 

time: 213 us -> 202 us (0.948); the launches traced: 210 us -> 202 us
  Pallas kernels: 207 us -> 199 us
    pallas_call x1, Pallas kernels: 207 us -> 199 us  [per_device(): pl.pallas_call(functools.partial(kernel, groups, hi, lo), out_shape=jax.S...]
where the time goes in v2:
time: 202 us
  Pallas kernels  199 us (99%)
    pallas_call x1, Pallas kernels, per_device(): pl.pallas_call(functools.partial(kernel, groups, hi, lo), out_shape=jax.S...  199 us

profile of v2, /device:TPU:2, one launch (start us, length us, event | category | flops | bytes accessed | tf_op | source)
XLA Modules:
  0.0 202.3 jit_solution(3310305291312826500)
XLA Ops:
  0.0 1.3 select_reduce_fusion.inv
  1.3 199.1 %shard_map.55 = f32[2,512,128]{2,1,0:T(8,128)} custom-call(s32[1,2]{1,0:T(1,128)} %sep.1, s32[2,32]{1,0:T(2,128)} %select_reduce_fusion.inv, f32[2,512,128]{2,1,0:T(8,128)} %bitcast.8, bf16[2,512,4096]{2,1,0:T(8,128)(2,1)} %bitcast.5, bf16[2,32,128,512]{3,2,1,0:T(8,128)(2,1)} %bitcast.6), custom_call_target="tpu_custom_call" | custom-call | tf_op jit(solution)/shard_map/pallas_call | solution.py:439
  200.4 1.9 copy.7

commit v3 on v2

--- a/solution.py
+++ b/solution.py
@@ -133,47 +133,58 @@
     def ag_lo(k, q, e, d):
         return remote(ag.at[k, q], ag.at[k, q], s_ag2.at[k, e, d], r_ag.at[k, q], (m, peer(e)))
 
-    def gather(k, consume):
+    def gather(k, consume, weight):
         for d in range(1, hi):
-            ag_hi(k, d).start()
+            pl.when(near(d) > h)(lambda: ag_hi(k, d).start())
         for e in range(1, lo):
             ag_lo(k, f, e, 0).start()
+        weight.wait()
         consume(f)
 
         def from_hi(d):
-            q = near(d) * lo + l
-            ag_lo(k, q, 0, 0).wait_recv()
-            for e in range(1, lo):
-                ag_lo(k, q, e, d).start()
-            consume(q)
+            @pl.when(near(d) < h)
+            def _():
+                q = near(d) * lo + l
+                ag_lo(k, q, 0, 0).wait_recv()
+                for e in range(1, lo):
+                    ag_lo(k, q, e, d).start()
+                consume(q)
 
         loop(1, hi, from_hi)
         for e in range(1, lo):
             def from_lo(d):
-                q = near(d) * lo + (l + lo - e) % lo
-                ag_lo(k, q, 0, 0).wait_recv()
-                consume(q)
+                @pl.when(near(d) <= h)
+                def _():
+                    q = near(d) * lo + (l + lo - e) % lo
+                    ag_lo(k, q, 0, 0).wait_recv()
+                    consume(q)
 
             loop(0, hi, from_lo)
 
     def gather_sent(k):
         for d in range(1, hi):
-            ag_hi(k, d).wait_send()
-        for e in range(1, lo):
-            loop(0, hi, lambda d: ag_lo(k, near(d) * lo + l, e, d).wait_send())
+            pl.when(near(d) > h)(lambda: ag_hi(k, d).wait_send())
+        for e in range(1, lo):
+            def forwarded(d):
+                pl.when(near(d) <= h)(lambda: ag_lo(k, near(d) * lo + l, e, d).wait_send())
+
+            loop(0, hi, forwarded)
 
     def rs1(st_, p_, s_, r_, k, e, h2):
         q = h2 * lo + (l + e) % lo
         return remote(st_.at[k, q], p_.at[k, e, h2], s_.at[k, e, h2], r_.at[k, e, h2], (m, peer(e)))
 
-    def reduce_lo(bufs, k, produce, finish, steps):
+    def reduce_lo(bufs, k, produce, finish, steps, needed=lambda h2: h2 >= 0):
         st_, p_, s_, r_ = bufs
         for e in range(1, lo):
             def send(d):
                 h2 = near((d + 1) % hi)
                 q = h2 * lo + (l + e) % lo
-                st_[k, q] = produce(q).astype(BF16)
-                rs1(st_, p_, s_, r_, k, e, h2).start()
+
+                @pl.when(needed(h2))
+                def _():
+                    st_[k, q] = produce(q).astype(BF16)
+                    rs1(st_, p_, s_, r_, k, e, h2).start()
 
             loop(0, hi, send)
 
@@ -186,16 +197,22 @@
 
         def body(d):
             h2 = near((d + 1) % hi)
-            st_[k, h2 * lo + l] = total(h2)
-            finish(h2)
+
+            @pl.when(needed(h2))
+            def _():
+                st_[k, h2 * lo + l] = total(h2)
+                finish(h2)
 
         loop(0, steps, body)
         return total
 
-    def reduce_sent(bufs, k):
+    def reduce_sent(bufs, k, needed=lambda h2: h2 >= 0):
         st_, p_, s_, r_ = bufs
         for e in range(1, lo):
-            loop(0, hi, lambda h2: rs1(st_, p_, s_, r_, k, e, h2).wait_send())
+            def gone(h2):
+                pl.when(needed(h2))(lambda: rs1(st_, p_, s_, r_, k, e, h2).wait_send())
+
+            loop(0, hi, gone)
 
     up = (st, p1, s_1, r_1)
     down = (stb, p1b, s_b1, r_b1)
@@ -222,12 +239,13 @@
 
     ag[0, f] = jnp.where(keep_rows(0), rhs[0], 0.0).astype(BF16)
     pl.semaphore_wait(barrier, count)
-    weights[0].wait()
-    gather(0, solve(0))
+    gather(0, solve(0), weights[0])
     leaf = jnp.where(keep_rows(0), acc[...], 0.0)
-    xs[0] = leaf.T
     xb[...] = leaf.astype(BF16)
     weights[1].wait()
+
+    def hold(k):
+        xs[k] = jnp.where(keep_rows(k), acc[...], 0.0).T
 
     def lifted(k):
         return lambda q: jnp.dot(blocks(k, q), xb[...], preferred_element_type=F32)
@@ -251,10 +269,12 @@
 
         total = reduce_lo(up, 0, produce, lambda h2: rs2(0, 0, m, h2).start(), hi - 1)
         p2[0, h] = total(h)
+        hold(0)
         loop(1, hi, lambda d: wait2(0, near(d)))
 
     @pl.when(jnp.logical_not(odd))
     def _():
+        hold(0)
         loop(0, hi, lambda h2: wait2(0, h2))
 
     incoming = p2[0, 0].astype(F32)
@@ -271,10 +291,8 @@
         acc[...] -= other
 
     ag[1, f] = jnp.where(keep_rows(1), acc[...], 0.0).astype(BF16)
-    weights[2].wait()
-    gather(1, solve(1))
+    gather(1, solve(1), weights[2])
     upper = jnp.where(keep_rows(1), acc[...], 0.0)
-    xs[1] = upper.T
     xb[...] = upper.astype(BF16)
     weights[3].wait()
 
@@ -294,10 +312,12 @@
         acct[...] += jnp.dot(agb[k, q], blocks(k, q), preferred_element_type=F32)
 
     acct[...] = jnp.zeros_like(acct)
+    pl.when(top)(lambda: hold(1))
 
     @pl.when(jnp.logical_not(top))
     def _():
         reduce_lo(up, 1, lifted(1), lambda h2: rs2(1, slot, parent, h2).start(), hi)
+        hold(1)
 
         def from_parent(d):
             q = near(d) * lo + l
@@ -321,19 +341,20 @@
         def produce(q):
             return jnp.dot(ab[...], columns(k, q), preferred_element_type=F32)
 
-        total = reduce_lo(down, k, produce, lambda h2: rs2b(k, h2).start(), hi - 1)
-        value = total(h).astype(F32)
-
-        def collect(d):
+        total = reduce_lo(down, k, produce, lambda h2: rs2b(k, h2).start(), hi - 1, lambda h2: h2 <= h)
+        acct[...] = total(h).astype(F32)
+
+        for d in range(1, hi):
             source = near(d)
-            remote(
-                p2b.at[k, source], p2b.at[k, source], s_b2.at[k, 0], r_b2.at[k, source], (mate, f)
-            ).wait_recv()
-            return p2b[k, source].astype(F32)
-
-        for d in range(1, hi):
-            value = value + collect(d)
-        return jnp.where(keep_columns(k), value, 0.0)
+
+            @pl.when(source > h)
+            def _():
+                remote(
+                    p2b.at[k, source], p2b.at[k, source], s_b2.at[k, 0], r_b2.at[k, source], (mate, f)
+                ).wait_recv()
+                acct[...] += p2b[k, source].astype(F32)
+
+        return jnp.where(keep_columns(k), acct[...], 0.0)
 
     solved = descend(1)
     zs[...] = solved.astype(BF16)
@@ -392,8 +413,9 @@
 
     for k in range(2):
         gather_sent(k)
-        reduce_sent(down, k)
-        loop(1, hi, lambda d: rs2b(k, (h + d) % hi).wait_send())
+        reduce_sent(down, k, lambda h2: h2 <= h)
+        for d in range(1, hi):
+            pl.when(near(d) < h)(lambda: rs2b(k, near(d)).wait_send())
 
     @pl.when(jnp.logical_not(top))
     def _():

time: 202 us -> 195 us (0.965)
  Pallas kernels: 199 us -> 192 us
    pallas_call x1, Pallas kernels: 199 us -> 192 us  [per_device(): pl.pallas_call(functools.partial(kernel, groups, hi, lo), out_shape=jax.S...]
where the time goes in v3:
time: 195 us
  Pallas kernels  192 us (98%)
    pallas_call x1, Pallas kernels, per_device(): pl.pallas_call(functools.partial(kernel, groups, hi, lo), out_shape=jax.S...  192 us

profile of v3, /device:TPU:2, one launch (start us, length us, event | category | flops | bytes accessed | tf_op | source)
XLA Modules:
  0.0 195.2 jit_solution(16256553694162510509)
XLA Ops:
  0.0 1.3 select_reduce_fusion.inv
  1.3 192.0 %shard_map.55 = f32[2,512,128]{2,1,0:T(8,128)} custom-call(s32[1,2]{1,0:T(1,128)} %sep.1, s32[2,32]{1,0:T(2,128)} %select_reduce_fusion.inv, f32[2,512,128]{2,1,0:T(8,128)} %bitcast.8, bf16[2,512,4096]{2,1,0:T(8,128)(2,1)} %bitcast.5, bf16[2,32,128,512]{3,2,1,0:T(8,128)(2,1)} %bitcast.6), custom_call_target="tpu_custom_call" | custom-call | tf_op jit(solution)/shard_map/pallas_call | solution.py:461
  193.3 1.9 copy.7
